TPU v7x, 256 devices: a whole 4x4x8 slice. The times are simulated.
256 devices in a mesh: rows: 64 (over z, y, core), grp: 4 (over x).
Axes of the slice: x: 4, y: 4, z: 8, core: 2. Of those that a mesh axis runs over, the one named last changes fastest.
Arguments:
- item_factors: bfloat16 [1048576, 128], P('rows'), may hold values from -120 to 120
- rated_owner: int32 [32768, 128], P(('rows', 'grp')), may hold values from 0 to 63, as said below
- rated_row: int32 [32768, 128], P(('rows', 'grp')), may hold values from 0 to 16383
- strength: float32 [32768, 128], P(('rows', 'grp')), may hold values from 0.1 to 3
Outputs:
- user_factors: float32 [32768, 128], P(('rows', 'grp'))
Inputs may be any that keep to these rules, and one draw needn't show every extreme that they name: `rated_owner`: among the 16384 slots of one device's users, at most 512 name one block; one block is named exactly 512 times by every device.
All inputs are finite; a program needn't handle non-finite values.
Results may differ from a plain program's by a relative error of at most 0.009.
Values may be sent and summed in bfloat16 or wider, within the bound.
A program may use at most 64 MiB of HBM per device.

v0:
```python
import jax
import jax.numpy as jnp
from jax import lax
from jax.sharding import PartitionSpec as P

ITERS = 16
USER_BLOCK = 16


ridge = 5.0
tiny = 1e-06


def conjugate(apply_system, target):

    def advance(index, carry):
        solution, residual, direction, norm_now = carry
        image = apply_system(direction)
        alpha = norm_now / (jnp.sum(direction * image, axis=1, keepdims=True) + tiny)
        solution = solution + alpha * direction
        residual = residual - alpha * image
        norm_next = jnp.sum(residual * residual, axis=1, keepdims=True)
        direction = residual + norm_next / (norm_now + tiny) * direction
        return (solution, residual, direction, norm_next)

    start = (
        jnp.zeros_like(target),
        target,
        target,
        jnp.sum(target * target, axis=1, keepdims=True),
    )
    result = lax.fori_loop(0, ITERS, advance, start)
    return result[0]


def per_device(item_factors, rated_owner, rated_row, strength):
    user_count, slot_count = rated_owner.shape
    shard_rows, rank = item_factors.shape
    owners_count = lax.axis_size("rows")
    slot_owner = rated_owner.reshape(-1)
    local_row = rated_row.reshape(-1)
    slot_total = slot_owner.shape[0]
    capacity = 2 * slot_total // owners_count
    slot_order = jnp.argsort(slot_owner, stable=True)
    sorted_owner = slot_owner[slot_order]
    owner_starts = jnp.searchsorted(sorted_owner, jnp.arange(owners_count, dtype=jnp.int32))
    sorted_rank = jnp.arange(slot_total, dtype=jnp.int32) - owner_starts[sorted_owner]
    sorted_place = sorted_owner * capacity + sorted_rank
    bucket_slot = jnp.zeros((slot_total,), jnp.int32).at[slot_order].set(sorted_place)
    asked_rows = jnp.zeros((owners_count * capacity,), jnp.int32).at[bucket_slot].set(local_row)
    asked_rows = asked_rows.reshape(owners_count, capacity)
    found = jnp.take(
        item_factors,
        lax.all_to_all(asked_rows, "rows", split_axis=0, concat_axis=0, tiled=True),
        axis=0,
    )
    fetched = lax.all_to_all(found, "rows", split_axis=0, concat_axis=0, tiled=True)
    slot_rows = jnp.take(fetched.reshape(owners_count * capacity, rank), bucket_slot, axis=0)
    copies = lax.axis_size("grp")
    share = shard_rows // copies
    piece = lax.dynamic_slice_in_dim(item_factors, lax.axis_index("grp") * share, share, 0)
    partial_gram = jnp.einsum("ir,it->rt", piece, piece, preferred_element_type=jnp.float32)
    gram_total = lax.psum(partial_gram, ("rows", "grp"))
    gram_mean = gram_total / (shard_rows * owners_count)
    gram_weighted = slot_count * gram_mean
    block_count = user_count // USER_BLOCK
    grouped_rows = slot_rows.reshape(block_count, USER_BLOCK, slot_count, rank)
    grouped_weights = strength.reshape(block_count, USER_BLOCK, slot_count)

    def solve_group(pair):
        rows_block, weight_block = pair
        rows_wide = rows_block.astype(jnp.float32)
        weighted = rows_wide * weight_block[:, :, None]
        target = jnp.sum(rows_wide + weighted, axis=1)
        system = gram_weighted[None] + jnp.einsum(
            "usr,ust->urt", weighted, rows_wide, precision=lax.Precision.HIGHEST
        )
        system = system + ridge * jnp.eye(rank, dtype=jnp.float32)[None]

        def apply_system(direction):
            return jnp.einsum("urt,ut->ur", system, direction, precision=lax.Precision.HIGHEST)

        return conjugate(apply_system, target)

    solved = lax.map(solve_group, (grouped_rows, grouped_weights))
    return solved.reshape(user_count, rank)


def solution(mesh):
    placed = (
        P("rows", None),
        P(("rows", "grp"), None),
        P(("rows", "grp"), None),
        P(("rows", "grp"), None),
    )
    return jax.shard_map(
        per_device, mesh=mesh, in_specs=placed, out_specs=P(("rows", "grp"), None), check_vma=False
    )
```

profile of v0, /device:TPU:1, one launch (start us, length us, event | category | flops | bytes accessed | tf_op | source)
XLA Modules:
  0.0 1135.9 jit_solution(973343675784601571)
XLA Ops:
  6.5 8.7 sort.17
  15.2 90.7 %gather_fusion.1 = s32[16384]{0:T(1024)S(1)} fusion(s32[16384]{0:T(1024)S(1)} %bitcast.141, s32[16384]{0:T(1024)S(1)} %get-tuple-element.268), kind=kCustom, calls=%fused_computation.1 | custom fusion | bytes 196608 | tf_op jit(solution)/shard_map/gather | solution.py:45
  106.0 12.4 %while.53 = (s32[]{:T(128)}, u32[64]{0:T(128)S(1)}, u32[64]{0:T(128)S(1)}, s32[16384]{0:T(1024)S(1)}, s32[]{:T(128)}, /*index=5*/s32[]{:T(128)}, s32[]{}) while((s32[]{:T(128)}, u32[64]{0:T(128)S(1)}, u32[64]{0:T(128)S(1)}, s32[16384]{0:T(1024)S(1)}, s32[]{:T(128)}, /*index=5*/s32[]{:T(128)}, s32[]{}) %tuple.194), condition=%wide.region_2.3_spmd.clone, body=%wide.region_1.2_spmd.clone.sunk | while | flops 1860 | bytes 7268 | solution.py:46
  121.2 4.5 compare_select_fusion.3
  125.8 13.6 %compare_reduce_fusion.56 = (pred[16384]{0:T(1024)(128)(4,1)S(1)}, pred[16384]{0:T(1024)(128)(4,1)S(1)}, pred[16384]{0:T(1024)(128)(4,1)S(1)}, pred[16384]{0:T(1...) fusion(s32[16384,1]{0,1:T(1,128)S(1)} %get-tuple-element.261), kind=kLoop, calls=%fused_computation.102 | loop fusion | flops 933888 | bytes 999424 | tf_op jit(solution)/shard_map/gather | solution.py:47
  139.4 36.3 %fusion.23 = s32[16384]{0:T(1024)S(1)} fusion(pred[16384]{0:T(1024)(128)(4,1)S(1)} %get-tuple-element.227, pred[16384]{0:T(1024)(128)(4,1)S(1)} %get-tuple-element.226, pred[16384]{0:T(1024)(128)(4,1)S(1)} %get-tuple-element.225, pred[16384]{0:T(1024)(128)(4,1)S(1)} %get-tuple-element.224, pred[16384]{0:T(1024)(128)(4,1)S(1)} %get-tuple-element.223, ...), kind=kLoop, calls=%fused_computation.114 | loop fusion | flops 983040 | bytes 1130724 | tf_op jit(solution)/shard_map/add | solution.py:48
  175.7 60.3 %scatter_custom_fusion = s32[16384]{0:T(1024)S(1)} fusion(s32[16384]{0:T(1024)S(1)} %get-tuple-element.269, s32[16384]{0:T(1024)S(1)} %fusion.23, s32[]{:T(128)} %constant.95.clone.1), kind=kCustom, calls=%fused_computation.121 | custom fusion | bytes 65540 | tf_op jit(solution)/shard_map/scatter | solution.py:49
  236.1 60.6 %scatter_custom_fusion.1 = s32[32768]{0:T(1024)S(1)} fusion(s32[16384]{0:T(1024)S(1)} %get-tuple-element.267, s32[16384]{0:T(1024)} %bitcast.155, s32[]{:T(128)} %constant.95.clone.1), kind=kCustom, calls=%fused_computation.115 | custom fusion | bytes 131584 | tf_op jit(solution)/shard_map/scatter | solution.py:50
  296.7 24.1 %all_to_all.20 = s32[64,1,512]{2,1,0:T(1,128)S(1)} all-to-all(s32[64,1,512]{2,1,0:T(1,128)S(1)} %bitcast.148), channel_id=1, replica_groups=mesh['rows'=64,'grp'=4] {'rows'}, dimensions={0} | all-to-all | bytes 262144 | tf_op jit(solution)/shard_map/all_to_all | solution.py:54
  320.9 112.1 %gather_fusion.2 = bf16[32768,128]{1,0:T(8,128)(2,1)} fusion(bf16[16384,128]{1,0:T(8,128)(2,1)} %param.10, s32[32768]{0:T(1024)S(1)} %broadcast_clamp_fusion), kind=kCustom, calls=%fused_computation.2 | custom fusion | bytes 16908288 | tf_op jit(solution)/shard_map/jit(_take)/gather | solution.py:52
  433.0 7.8 broadcast_select_fusion.2
  440.8 5.7 all-to-all-start.1
  446.6 2.8 fusion.21
  449.5 297.3 %all-reduce.2.cloned.1.call-done = f32[128,128]{1,0:T(8,128)} async-done(((f32[128,128]{1,0:T(8,128)}), f32[128,128]{1,0:T(8,128)}) %all-reduce.2.cloned.1.call-update) | async-done | bytes 65552 | tf_op jit(solution)/shard_map/psum | solution.py:63
  747.6 59.4 %gather_fusion.3 = bf16[16384,128]{1,0:T(8,128)(2,1)} fusion(bf16[32768,128]{1,0:T(8,128)(2,1)} %bitcast.77, s32[16384]{0:T(1024)S(1)} %get-tuple-element.266), kind=kCustom, calls=%fused_computation.3 | custom fusion | bytes 8454144 | tf_op jit(solution)/shard_map/jit(_take)/gather | solution.py:58
  807.0 7.6 broadcast_select_fusion.3
  814.6 313.8 %while.52 = (s32[]{:T(128)}, f32[8,16,128]{2,1,0:T(8,128)S(1)}, bf16[8,16,128,128]{3,2,1,0:T(8,128)(2,1)}, f32[8,16,128]{2,1,0:T(8,128)}, f32[128,128]{1,0:T(8,1...) while((s32[]{:T(128)}, f32[8,16,128]{2,1,0:T(8,128)S(1)}, bf16[8,16,128,128]{3,2,1,0:T(8,128)(2,1)}, ...), condition=%wide.region_13.14_spmd, body=%wide.region_6.13_spmd.sunk | while | flops 407953440 | bytes 4049040 | solution.py:85
  816.9 2.5 fusion.51
  819.4 34.5 %while.54 = (s32[]{:T(128)}, f32[16,128]{1,0:T(8,128)S(1)}, f32[16,128]{1,0:T(8,128)S(1)}, f32[16,128]{1,0:T(8,128)S(1)}, f32[16,1]{0,1:T(1,128)S(1)}, /*index=5*/f32[16,128,128]{2,1,0:T(8,128)S(1)}, s32[]{:T(128)}, s32[]{:T(128)}) while((s32[]{:T(128)}, f32[16,128]{1,0:T(8,128)S(1)}, f32[16,128]{1,0:T(8,128)S(1)}, ...), condition=%wide.region_12.12_spmd.clone, body=%wide.region_9.11_spmd.clone.sunk | while | flops 3168291 | bytes 1147807 | solution.py:32
  821.5 1.7 fusion.55
  836.6 1.7 fusion.55
  851.7 1.7 fusion.55
  856.1 2.5 fusion.51
  858.6 34.5 %while.54 = (s32[]{:T(128)}, f32[16,128]{1,0:T(8,128)S(1)}, f32[16,128]{1,0:T(8,128)S(1)}, f32[16,128]{1,0:T(8,128)S(1)}, f32[16,1]{0,1:T(1,128)S(1)}, /*index=5*/f32[16,128,128]{2,1,0:T(8,128)S(1)}, s32[]{:T(128)}, s32[]{:T(128)}) while((s32[]{:T(128)}, f32[16,128]{1,0:T(8,128)S(1)}, f32[16,128]{1,0:T(8,128)S(1)}, ...), condition=%wide.region_12.12_spmd.clone, body=%wide.region_9.11_spmd.clone.sunk | while | flops 3168291 | bytes 1147807 | solution.py:32
  869.4 1.7 fusion.55
  884.4 1.7 fusion.55
  895.3 2.5 fusion.51
  897.8 34.5 %while.54 = (s32[]{:T(128)}, f32[16,128]{1,0:T(8,128)S(1)}, f32[16,128]{1,0:T(8,128)S(1)}, f32[16,128]{1,0:T(8,128)S(1)}, f32[16,1]{0,1:T(1,128)S(1)}, /*index=5*/f32[16,128,128]{2,1,0:T(8,128)S(1)}, s32[]{:T(128)}, s32[]{:T(128)}) while((s32[]{:T(128)}, f32[16,128]{1,0:T(8,128)S(1)}, f32[16,128]{1,0:T(8,128)S(1)}, ...), condition=%wide.region_12.12_spmd.clone, body=%wide.region_9.11_spmd.clone.sunk | while | flops 3168291 | bytes 1147807 | solution.py:32
  902.1 1.7 fusion.55
  917.2 1.7 fusion.55
  934.5 2.5 fusion.51
  937.1 34.5 %while.54 = (s32[]{:T(128)}, f32[16,128]{1,0:T(8,128)S(1)}, f32[16,128]{1,0:T(8,128)S(1)}, f32[16,128]{1,0:T(8,128)S(1)}, f32[16,1]{0,1:T(1,128)S(1)}, /*index=5*/f32[16,128,128]{2,1,0:T(8,128)S(1)}, s32[]{:T(128)}, s32[]{:T(128)}) while((s32[]{:T(128)}, f32[16,128]{1,0:T(8,128)S(1)}, f32[16,128]{1,0:T(8,128)S(1)}, ...), condition=%wide.region_12.12_spmd.clone, body=%wide.region_9.11_spmd.clone.sunk | while | flops 3168291 | bytes 1147807 | solution.py:32
  945.7 1.7 fusion.55
  973.8 2.5 fusion.51
  976.3 34.5 %while.54 = (s32[]{:T(128)}, f32[16,128]{1,0:T(8,128)S(1)}, f32[16,128]{1,0:T(8,128)S(1)}, f32[16,128]{1,0:T(8,128)S(1)}, f32[16,1]{0,1:T(1,128)S(1)}, /*index=5*/f32[16,128,128]{2,1,0:T(8,128)S(1)}, s32[]{:T(128)}, s32[]{:T(128)}) while((s32[]{:T(128)}, f32[16,128]{1,0:T(8,128)S(1)}, f32[16,128]{1,0:T(8,128)S(1)}, ...), condition=%wide.region_12.12_spmd.clone, body=%wide.region_9.11_spmd.clone.sunk | while | flops 3168291 | bytes 1147807 | solution.py:32
  978.4 1.7 fusion.55
  1004.3 1.7 fusion.55
  1013.0 2.5 fusion.51
  1015.5 34.5 %while.54 = (s32[]{:T(128)}, f32[16,128]{1,0:T(8,128)S(1)}, f32[16,128]{1,0:T(8,128)S(1)}, f32[16,128]{1,0:T(8,128)S(1)}, f32[16,1]{0,1:T(1,128)S(1)}, /*index=5*/f32[16,128,128]{2,1,0:T(8,128)S(1)}, s32[]{:T(128)}, s32[]{:T(128)}) while((s32[]{:T(128)}, f32[16,128]{1,0:T(8,128)S(1)}, f32[16,128]{1,0:T(8,128)S(1)}, ...), condition=%wide.region_12.12_spmd.clone, body=%wide.region_9.11_spmd.clone.sunk | while | flops 3168291 | bytes 1147807 | solution.py:32
  1017.7 1.7 fusion.55
  1032.8 1.7 fusion.55
  1052.2 2.5 fusion.51
  1054.8 34.5 %while.54 = (s32[]{:T(128)}, f32[16,128]{1,0:T(8,128)S(1)}, f32[16,128]{1,0:T(8,128)S(1)}, f32[16,128]{1,0:T(8,128)S(1)}, f32[16,1]{0,1:T(1,128)S(1)}, /*index=5*/f32[16,128,128]{2,1,0:T(8,128)S(1)}, s32[]{:T(128)}, s32[]{:T(128)}) while((s32[]{:T(128)}, f32[16,128]{1,0:T(8,128)S(1)}, f32[16,128]{1,0:T(8,128)S(1)}, ...), condition=%wide.region_12.12_spmd.clone, body=%wide.region_9.11_spmd.clone.sunk | while | flops 3168291 | bytes 1147807 | solution.py:32
  1065.5 1.7 fusion.55
  1091.4 2.5 fusion.51
  1094.0 34.5 %while.54 = (s32[]{:T(128)}, f32[16,128]{1,0:T(8,128)S(1)}, f32[16,128]{1,0:T(8,128)S(1)}, f32[16,128]{1,0:T(8,128)S(1)}, f32[16,1]{0,1:T(1,128)S(1)}, /*index=5*/f32[16,128,128]{2,1,0:T(8,128)S(1)}, s32[]{:T(128)}, s32[]{:T(128)}) while((s32[]{:T(128)}, f32[16,128]{1,0:T(8,128)S(1)}, f32[16,128]{1,0:T(8,128)S(1)}, ...), condition=%wide.region_12.12_spmd.clone, body=%wide.region_9.11_spmd.clone.sunk | while | flops 3168291 | bytes 1147807 | solution.py:32
  1098.3 1.7 fusion.55
  1124.1 1.7 fusion.55
  (1020 shorter events, 280.3 us)
Async XLA Ops:
  6.5 8.7 copy-start
  440.8 306.8 %all-to-all-start.1 = ((bf16[64,512,128]{2,1,0:T(8,128)(2,1)}), bf16[64,512,128]{2,1,0:T(8,128)(2,1)}, u32[]{:S(2)}, u32[]{:S(2)}) async-start(bf16[64,512,128]{2,1,0:T(8,128)(2,1)} %broadcast_select_fusion.2), calls=%async_computation.1 | async-start | bytes 16777216 | tf_op jit(solution)/shard_map/all_to_all | solution.py:57
  446.6 300.2 %all-reduce.2.cloned.1.call-start = ((), (), s32[]{:S(2)}) async-start(), calls=%async_computation.2 | async-start | bytes 131072 | tf_op jit(solution)/shard_map/psum | solution.py:63
  1128.4 0.6 copy-start.1
Sparse Core Ops, SparseCore 0:
  452.9 293.8 all-reduce.1
where the time goes:
time: 1140 us
  local copies, waits for them, and re-layouts  404 us (35%)
  waiting for transfers between devices  297 us (26%)
  matrix products  244 us (21%)
  other arithmetic  143 us (13%)
  blocking collectives  24.1 us (2%)
  between operations  13.5 us (1%)
    psum x1, waiting for transfers between devices, per_device(): gram_total = lax.psum(partial_gram, ('rows', 'grp'))  297 us
    dot_general x128, matrix products, apply_system(): jnp.einsum('urt,ut->ur', system, direction, precision=lax.Precision.HIGHEST)  221 us
    gather x1, local copies, waits for them, and re-layouts, per_device(): jnp.take(item_factors, lax.all_to_all(asked_rows, 'rows', split_axis=0, c...  112 us
    gather x1, local copies, waits for them, and re-layouts, per_device(): sorted_owner = slot_owner[slot_order]  90.7 us
    scatter x1, local copies, waits for them, and re-layouts, per_device(): jnp.zeros((owners_count * capacity,), jnp.int32).at[bucket_slot]  60.6 us
    scatter x1, local copies, waits for them, and re-layouts, per_device(): jnp.zeros((slot_total,), jnp.int32).at[slot_order].set(sorted_place)  60.3 us
    gather x1, local copies, waits for them, and re-layouts, per_device(): jnp.take(fetched.reshape(owners_count * capacity, rank), bucket_slot, axi...  59.4 us
    add x1, other arithmetic, per_device(): sorted_place = sorted_owner * capacity + sorted_rank  36.3 us
  transfers between devices with their start and end apart: 2, of which 1 were waited for; matrix products, arithmetic and copies ran while one was open for 0% of the time, Pallas kernels for 0%

commit v1 on v0

v1 whole, which is shorter than its diff:
```python
import functools
import jax
import jax.numpy as jnp
from jax import lax
from jax.experimental import pallas as pl
from jax.experimental.pallas import tpu as pltpu
from jax.sharding import PartitionSpec as P

f32, bf16, i32 = jnp.float32, jnp.bfloat16, jnp.int32
ITERS = 16
ridge = 5.0
tiny = 1e-6
MIB = 1024 * 1024


def prep_kernel(owners, cap, group, owner_ref, row_ref, place_ref, asked_ref, base, acc):
    users, slots = owner_ref.shape
    which = lax.broadcasted_iota(i32, (owners, slots), 0)
    before = lax.broadcasted_iota(i32, (slots, 2 * slots), 0)
    after = lax.broadcasted_iota(i32, (slots, 2 * slots), 1)
    earlier = jnp.where((before < after) | (after >= slots), 1.0, 0.0).astype(bf16)
    ranks = lax.broadcasted_iota(i32, (cap, slots), 0)
    base[...] = jnp.zeros_like(base)
    acc[...] = jnp.zeros_like(acc)

    def step(index, _):
        left, right = [], []
        for inner in range(group):
            user = index * group + inner
            own = owner_ref[pl.ds(user, 1), :]
            row = row_ref[pl.ds(user, 1), :]
            hot = jnp.where(which == own, 1.0, 0.0)
            counts = jnp.dot(hot.astype(bf16), earlier, preferred_element_type=f32)
            rank = jnp.sum(hot * (counts[:, :slots] + base[...]), axis=0, keepdims=True).astype(i32)
            base[...] += counts[:, slots:]
            place_ref[pl.ds(user, 1), :] = own * cap + rank
            high = (row // 128).astype(f32)
            low = (row % 128).astype(f32)
            left.append(jnp.concatenate([hot * high, hot * low], axis=0).astype(bf16))
            right.append(jnp.where(ranks == rank, 1.0, 0.0).astype(bf16))
        acc[...] += lax.dot_general(
            jnp.concatenate(left, axis=1),
            jnp.concatenate(right, axis=1),
            (((1,), (1,)), ((), ())),
            preferred_element_type=f32,
        )
        return 0

    lax.fori_loop(0, users // group, step, 0)
    total = acc[...]
    asked_ref[...] = (total[:owners] * 128.0 + total[owners:]).astype(i32)


def prepare(owner, row, owners, cap, group=16):
    users, slots = owner.shape
    return pl.pallas_call(
        functools.partial(prep_kernel, owners, cap, group),
        out_shape=(
            jax.ShapeDtypeStruct((users, slots), i32),
            jax.ShapeDtypeStruct((owners, cap), i32),
        ),
        in_specs=[pl.BlockSpec(memory_space=pltpu.VMEM)] * 2,
        out_specs=[pl.BlockSpec(memory_space=pltpu.VMEM)] * 2,
        scratch_shapes=[pltpu.VMEM((owners, slots), f32), pltpu.VMEM((2 * owners, cap), f32)],
        compiler_params=pltpu.CompilerParams(vmem_limit_bytes=32 * MIB),
    )(owner, row)


def split3(x):
    high = x.astype(bf16)
    rest = x - high.astype(f32)
    mid = rest.astype(bf16)
    low = (rest - mid.astype(f32)).astype(bf16)
    return high, mid, low


def conjugate(big, target, vec):
    rank, users = target.shape

    def apply_system():
        def part(index, acc):
            return acc + big[pl.ds(pl.multiple_of(index * rank, rank), rank), :] * vec[pl.ds(index, 1), :]
        return lax.fori_loop(0, rank, part, jnp.zeros((rank, users), f32), unroll=8)

    def advance(index, carry):
        solution, residual, norm_now = carry
        image = apply_system()
        direction = vec[...]
        alpha = norm_now / (jnp.sum(direction * image, axis=0, keepdims=True) + tiny)
        solution = solution + alpha * direction
        residual = residual - alpha * image
        norm_next = jnp.sum(residual * residual, axis=0, keepdims=True)
        vec[...] = residual + norm_next / (norm_now + tiny) * direction
        return solution, residual, norm_next

    vec[...] = target
    start = (jnp.zeros_like(target), target, jnp.sum(target * target, axis=0, keepdims=True))
    return lax.fori_loop(0, ITERS, advance, start)[0]


def solve_kernel(place, fetched, strength, gram, out, wide, rows, systems, big, targets, vec):
    users, slots = strength.shape
    rank = out.shape[1]
    fetch_total = wide.shape[0]
    step = 512

    def widen(index, _):
        at = pl.ds(pl.multiple_of(index * step, step), step)
        wide[at, :] = fetched[at, :].astype(f32)
        return 0

    lax.fori_loop(0, fetch_total // step, widen, 0)
    eye = jnp.where(
        lax.broadcasted_iota(i32, (rank, rank), 0) == lax.broadcasted_iota(i32, (rank, rank), 1), ridge, 0.0
    )
    shared = gram[...] + eye


    def some_users(index, _):
        helds = []
        for g in range(8):
            user = index * 8 + g
            for slot in range(slots):
                rows[pl.ds(g * slots + slot, 1), :] = wide[pl.ds(place[user * slots + slot], 1), :]
        for g in range(8):
            user = index * 8 + g
            held = rows[g * slots:(g + 1) * slots, :]
            short = held.astype(bf16)
            weights = strength[pl.ds(user, 1), :]
            turned = short.T.astype(f32)
            parts = split3(turned * weights)[:3]
            extra = split3(jnp.broadcast_to(1.0 + weights, (16, slots)))
            left = jnp.concatenate([*parts, *extra], axis=0)
            product = jnp.dot(left, short, preferred_element_type=f32)
            system = product[(3 - 1) * rank:3 * rank]
            for k in range(3 - 2, -1, -1):
                system = system + product[k * rank:(k + 1) * rank]
            systems[pl.ds(pl.multiple_of(user * rank, rank), rank), :] = system + shared
            tail = 3 * rank
            targets[pl.ds(user, 1), :] = (
                product[tail:tail + 1] + (product[tail + 16:tail + 17] + product[tail + 32:tail + 33])
            )
        return 0

    lax.fori_loop(0, users // 8, some_users, 0)

    def turn(index, _):
        block = systems[pl.ds(index, users, stride=rank), :]
        big[pl.ds(pl.multiple_of(index * rank, rank), rank), :] = block.T
        return 0

    lax.fori_loop(0, rank, turn, 0, unroll=8)
    out[...] = conjugate(big, targets[...].T, vec).T


def solve(place, fetched, strength, gram):
    users, slots = strength.shape
    total, rank = fetched.shape
    vmem = pl.BlockSpec(memory_space=pltpu.VMEM)
    return pl.pallas_call(
        solve_kernel,
        out_shape=jax.ShapeDtypeStruct((users, rank), f32),
        in_specs=[pl.BlockSpec(memory_space=pltpu.SMEM), vmem, vmem, vmem],
        out_specs=vmem,
        scratch_shapes=[
            pltpu.VMEM((total, rank), f32),
            pltpu.VMEM((8 * slots, rank), f32),
            pltpu.VMEM((users * rank, rank), f32),
            pltpu.VMEM((rank * rank, users), f32),
            pltpu.VMEM((users, rank), f32),
            pltpu.VMEM((rank, users), f32),
        ],
        compiler_params=pltpu.CompilerParams(vmem_limit_bytes=60 * MIB),
    )(place, fetched, strength, gram)


MESH = pl.DeviceIdType.MESH
LANES = 128


def exchange_kernel(cap, order, asked, table, out, got, idx, wide, block, send,
                    ask_send, ask_recv, idx_sem, row_send, row_recv, own_sem):
    me = lax.axis_index("rows")
    n = asked.shape[0]
    z, y, c = me // 8, (me // 2) % 4, me % 2

    def offset(step):
        if order == "zslow":
            return step // 8, (step // 2) % 4, step % 2
        if order == "pair":
            k = step % 8
            dz = (k + 1) // 2 * (1 - 2 * (k % 2))
            return (dz + 8) % 8, (step // 8) % 4, step // 32
        if order == "zfast":
            return step % 8, (step // 8) % 4, step // 32

    def ahead(step):
        dz, dy, dc = offset(step)
        return (((z + dz) % 8) * 4 + (y + dy) % 4) * 2 + (c + dc) % 2

    def behind(step):
        dz, dy, dc = offset(step)
        return (((z + 8 - dz) % 8) * 4 + (y + 4 - dy) % 4) * 2 + (c + 2 - dc) % 2

    barrier = pltpu.get_barrier_semaphore()

    def greet(step, _):
        pl.semaphore_signal(barrier, inc=1, device_id={"rows": ahead(step)}, device_id_type=MESH)
        return 0

    lax.fori_loop(1, n, greet, 0)
    pl.semaphore_wait(barrier, n - 1)

    def ask(step):
        return pltpu.make_async_remote_copy(
            src_ref=asked.at[ahead(step)], dst_ref=got.at[step], send_sem=ask_send.at[step],
            recv_sem=ask_recv.at[step], device_id={"rows": ahead(step)}, device_id_type=MESH)

    def ask_start(step, _):
        ask(step).start()
        return 0

    lax.fori_loop(1, n, ask_start, 0)

    part = 512

    def widen(index, _):
        at = pl.ds(pl.multiple_of(index * part, part), part)
        wide[at, :] = table[at, :].astype(f32)
        return 0

    lax.fori_loop(0, table.shape[0] // part, widen, 0)

    def fetch(slot, home):
        def rows(line, _):
            for inner in range(LANES):
                block[pl.ds(inner, 1), :] = wide[pl.ds(idx[slot, line, inner], 1), :]
            send[home, pl.ds(pl.multiple_of(line * LANES, LANES), LANES), :] = block[...].astype(bf16)
            return 0
        lax.fori_loop(0, cap // LANES, rows, 0)

    def answer(step):
        return pltpu.make_async_remote_copy(
            src_ref=send.at[step], dst_ref=out.at[me], send_sem=row_send.at[step],
            recv_sem=row_recv.at[step], device_id={"rows": behind(step)}, device_id_type=MESH)

    mine = pltpu.make_async_copy(asked.at[me], got.at[0], own_sem)
    mine.start()

    def asked_all(step, _):
        ask(step).wait_recv()
        return 0

    lax.fori_loop(1, n, asked_all, 0)
    mine.wait()
    numbers = pltpu.make_async_copy(got, idx, idx_sem)
    numbers.start()
    numbers.wait()

    def serve(step, _):
        fetch(step, step)
        answer(step).start()
        return 0

    lax.fori_loop(1, n, serve, 0)
    fetch(0, 0)
    own = pltpu.make_async_copy(send.at[0], out.at[me], own_sem)
    own.start()

    def finish(step, _):
        ask(step).wait_send()
        answer(step).wait_send()
        pltpu.make_async_remote_copy(
            src_ref=send.at[step], dst_ref=out.at[ahead(step)], send_sem=row_send.at[step],
            recv_sem=row_recv.at[step], device_id={"rows": ahead(step)}, device_id_type=MESH).wait_recv()
        return 0

    lax.fori_loop(1, n, finish, 0)
    own.wait()


def exchange(asked, table, order="pair", cid=0):
    owners, cap = asked.shape
    rows, rank = table.shape
    vmem = pl.BlockSpec(memory_space=pltpu.VMEM)
    dma = pltpu.SemaphoreType.DMA
    lines = cap // 128
    return pl.pallas_call(
        functools.partial(exchange_kernel, cap, order),
        out_shape=jax.ShapeDtypeStruct((owners, cap, rank), bf16),
        in_specs=[vmem, vmem],
        out_specs=pl.BlockSpec(memory_space=pl.ANY),
        scratch_shapes=[
            pltpu.VMEM((owners, lines, 128), i32),
            pltpu.SMEM((owners, lines, 128), i32),
            pltpu.VMEM((rows, rank), f32),
            pltpu.VMEM((LANES, rank), f32),
            pltpu.VMEM((owners, cap, rank), bf16),
            dma((owners,)), dma((owners,)), dma, dma((owners,)), dma((owners,)), dma,
        ],
        compiler_params=pltpu.CompilerParams(collective_id=cid, has_side_effects=True, vmem_limit_bytes=48 * MIB),
    )(asked.reshape(owners, lines, 128), table)


def per_device(item_factors, rated_owner, rated_row, strength):
    user_count, slot_count = rated_owner.shape
    shard_rows, rank = item_factors.shape
    owners = lax.axis_size("rows")
    cap = 2 * user_count * slot_count // owners
    place, asked = prepare(rated_owner, rated_row, owners, cap)
    copies = lax.axis_size("grp")
    share = shard_rows // copies
    piece = lax.dynamic_slice_in_dim(item_factors, lax.axis_index("grp") * share, share, 0)
    partial_gram = jnp.einsum("ir,it->rt", piece, piece, preferred_element_type=jnp.float32)
    gram_total = lax.psum(partial_gram, ("rows", "grp"))
    gram_weighted = slot_count * (gram_total / (shard_rows * owners))
    fetched = exchange(asked, item_factors)
    return solve(place.reshape(-1), fetched.reshape(owners * cap, rank), strength, gram_weighted)


def solution(mesh):
    placed = (P("rows", None), P(("rows", "grp"), None), P(("rows", "grp"), None), P(("rows", "grp"), None))
    return jax.shard_map(
        per_device, mesh=mesh, in_specs=placed, out_specs=P(("rows", "grp"), None), check_vma=False
    )
```

time: 1140 us -> 386 us (0.34)
  local copies, waits for them, and re-layouts: 404 us -> 4.51 us
  Pallas kernels: 0 us -> 275 us
  matrix products: 244 us -> 2.68 us
  waiting for transfers between devices: 297 us -> 88.6 us
  other arithmetic: 143 us -> 1.47 us
  blocking collectives: 24.1 us -> 0 us
    gather x22 -> x0, local copies, waits for them, and re-layouts: 277 us -> none  [the longest x1 112 us: per_device(): jnp.take(item_factors, lax.all_to_all(asked_rows, 'rows', split_axis=0, c...]
    pallas_call x0 -> x3, Pallas kernels: none -> 275 us  [the longest x1 223 us: exchange(): pl.pallas_call(functools.partial(exchange_kernel, cap, order), out_shape=...]
    dot_general x136 -> x0, matrix products: 241 us -> none  [the longest x128 221 us: apply_system(): jnp.einsum('urt,ut->ur', system, direction, precision=lax.Precision.HIGHEST)]
    psum x1, waiting for transfers between devices: 297 us -> 88.6 us  [per_device(): gram_total = lax.psum(partial_gram, ('rows', 'grp'))]
    scatter x2 -> x0, local copies, waits for them, and re-layouts: 121 us -> none  [the longest x1 60.6 us: per_device(): jnp.zeros((owners_count * capacity,), jnp.int32).at[bucket_slot]]
    reduce_sum x272 -> x0, other arithmetic: 51.2 us -> none  [the longest x128 23.6 us: advance(): norm_next = jnp.sum(residual * residual, axis=1, keepdims=True)]
    add x144 -> x0, other arithmetic: 46.1 us -> none  [the longest x1 36.3 us: per_device(): sorted_place = sorted_owner * capacity + sorted_rank]
    all_to_all x1 -> x0, blocking collectives: 24.1 us -> none  [per_device(): lax.all_to_all(asked_rows, 'rows', split_axis=0, concat_axis=0, tiled=True)]
  transfers between devices with their start and end apart: 2 -> 1, of which waited for: 1 -> 1; matrix products, arithmetic and copies ran while one was open for 0% -> 0% of each run, Pallas kernels for 0% -> 60%
where the time goes in v1:
time: 386 us
  Pallas kernels  275 us (71%)
  waiting for transfers between devices  88.6 us (23%)
  between operations  13.4 us (3%)
  local copies, waits for them, and re-layouts  4.51 us (1%)
    pallas_call x1, Pallas kernels, exchange(): pl.pallas_call(functools.partial(exchange_kernel, cap, order), out_shape=...  223 us
    psum x1, waiting for transfers between devices, per_device(): gram_total = lax.psum(partial_gram, ('rows', 'grp'))  88.6 us
    pallas_call x1, Pallas kernels, solve(): pl.pallas_call(solve_kernel, out_shape=jax.ShapeDtypeStruct((users, rank)...  43.8 us
    pallas_call x1, Pallas kernels, prepare(): pl.pallas_call(functools.partial(prep_kernel, owners, cap, group), out_sh...  8.46 us
  transfers between devices with their start and end apart: 1, of which 1 were waited for; matrix products, arithmetic and copies ran while one was open for 0% of the time, Pallas kernels for 60%

profile of v1, /device:TPU:1, one launch (start us, length us, event | category | flops | bytes accessed | tf_op | source)
XLA Modules:
  0.0 385.6 jit_solution(2878887265650035953)
XLA Ops:
  6.5 0.0 all-reduce.2.cloned.1.call-start
  6.5 2.7 fusion
  9.2 0.0 all-reduce.2.cloned.1.call-update
  9.2 0.0 copy-start.2
  9.3 0.8 copy-done.2
  10.1 0.0 copy-start.3
  10.1 0.8 copy-done.3
  10.9 8.5 %shard_map.46 = (s32[128,128]{1,0:T(8,128)S(1)}, s32[64,512]{1,0:T(8,128)S(1)}) custom-call(s32[128,128]{1,0:T(8,128)S(1)} %copy-done.2, s32[128,128]{1,0:T(8,128)S(1)} %copy-done.3), custom_call_target="tpu_custom_call" | custom-call | tf_op jit(solution)/shard_map/pallas_call | solution.py:56
  19.4 0.0 copy-start.1
  19.4 0.6 copy-done.1
  20.1 0.0 copy-start
  20.1 2.2 copy-done
  22.3 222.6 %shard_map.47 = bf16[64,512,128]{2,1,0:T(8,128)(2,1)} custom-call(s32[64,4,128]{2,1,0:T(4,128)S(1)} %reshape.10.asked, bf16[16384,128]{1,0:T(8,128)(2,1)S(1)} %copy-done), custom_call_target="tpu_custom_call" | custom-call | tf_op jit(solution)/shard_map/pallas_call | solution.py:288
  244.9 88.6 %all-reduce.2.cloned.1.call-done = f32[128,128]{1,0:T(8,128)} async-done(((f32[128,128]{1,0:T(8,128)}), f32[128,128]{1,0:T(8,128)}) %all-reduce.2.cloned.1.call-update) | async-done | bytes 65552 | tf_op jit(solution)/shard_map/psum | solution.py:315
  333.5 1.5 broadcast_multiply_fusion.gram
  335.0 43.8 %shard_map.48 = f32[128,128]{1,0:T(8,128)} custom-call(s32[16384]{0:T(1024)} %bitcast.2, bf16[32768,128]{1,0:T(8,128)(2,1)} %bitcast.3, f32[128,128]{1,0:T(8,128)} %strength.1, f32[128,128]{1,0:T(8,128)} %broadcast_multiply_fusion.gram), custom_call_target="tpu_custom_call" | custom-call | tf_op jit(solution)/shard_map/pallas_call | solution.py:160
  (1 shorter events, 0.0 us)
Async XLA Ops:
  6.5 327.0 %all-reduce.2.cloned.1.call-start = ((), (), s32[]{:S(2)}) async-start(), calls=%async_computation | async-start | bytes 131072 | tf_op jit(solution)/shard_map/psum | solution.py:315
  9.2 0.8 copy-start.2
  10.1 0.8 copy-start.3
  19.4 0.6 copy-start.1
  20.1 2.2 copy-start
Sparse Core Ops, SparseCore 0:
  12.9 320.5 all-reduce.1

commit v2 on v1

v2 whole, which is shorter than its diff:
```python
import functools
import jax
import jax.numpy as jnp
from jax import lax
from jax.experimental import pallas as pl
from jax.experimental.pallas import tpu as pltpu
from jax.sharding import PartitionSpec as P

f32, bf16, i32 = jnp.float32, jnp.bfloat16, jnp.int32
ITERS = 16
ridge = 5.0
tiny = 1e-6
MIB = 1024 * 1024


CAP_PART = 5
NEAR = 24


def prep_kernel(owners, cap, spare, group, owner_ref, row_ref, place_ref, asked_ref, hot_ref, wrong_ref, base, acc, ranks):
    users, slots = owner_ref.shape
    full = cap + spare
    which = lax.broadcasted_iota(i32, (owners, slots), 0)
    before = lax.broadcasted_iota(i32, (slots, 2 * slots), 0)
    after = lax.broadcasted_iota(i32, (slots, 2 * slots), 1)
    earlier = jnp.where((before < after) | (after >= slots), 1.0, 0.0).astype(bf16)
    base[...] = jnp.zeros_like(base)
    acc[...] = jnp.zeros_like(acc)
    columns = lax.broadcasted_iota(i32, (full, slots), 0)

    def step(index, _):
        left, right = [], []
        for inner in range(group):
            user = index * group + inner
            own = owner_ref[pl.ds(user, 1), :]
            row = row_ref[pl.ds(user, 1), :]
            named = jnp.where(which == own, 1.0, 0.0)
            counts = jnp.dot(named.astype(bf16), earlier, preferred_element_type=f32)
            rank = jnp.sum(named * (counts[:, :slots] + base[...]), axis=0, keepdims=True).astype(i32)
            base[...] += counts[:, slots:]
            ranks[pl.ds(user, 1), :] = rank
            high = (row // 128).astype(f32)
            low = (row % 128).astype(f32)
            left.append(jnp.concatenate([named * high, named * low], axis=0).astype(bf16))
            right.append(jnp.where(columns == rank, 1.0, 0.0).astype(bf16))
        acc[...] += lax.dot_general(
            jnp.concatenate(left, axis=1),
            jnp.concatenate(right, axis=1),
            (((1,), (1,)), ((), ())),
            preferred_element_type=f32,
        )
        return 0

    lax.fori_loop(0, users // group, step, 0)
    counts = base[...].astype(i32)
    hot = jnp.min(jnp.where(counts == jnp.max(counts), which, owners))
    hot_ref[0, 0] = hot
    own, rank = owner_ref[...], ranks[...]
    past = rank >= cap
    place_ref[...] = jnp.where(past & (own == hot), owners * cap - cap + rank, own * cap + jnp.minimum(rank, cap - 1))
    bad = jnp.sum(jnp.where(past & (own != hot), 1.0, 0.0))
    wrong_ref[...] = jnp.zeros_like(wrong_ref) + bad
    total = acc[...]
    asked = (total[:owners] * 128.0 + total[owners:]).astype(i32)
    for line in range(full // 128):
        asked_ref[:, line, :] = asked[:, line * 128:(line + 1) * 128]


def prepare(owner, row, owners, cap, spare, group=16):
    users, slots = owner.shape
    full = cap + spare
    vmem = pl.BlockSpec(memory_space=pltpu.VMEM)
    return pl.pallas_call(
        functools.partial(prep_kernel, owners, cap, spare, group),
        out_shape=(
            jax.ShapeDtypeStruct((users, slots), i32),
            jax.ShapeDtypeStruct((owners, full // 128, 128), i32),
            jax.ShapeDtypeStruct((1, 1), i32),
            jax.ShapeDtypeStruct((8, slots), f32),
        ),
        in_specs=[vmem, vmem],
        out_specs=(vmem, vmem, pl.BlockSpec(memory_space=pltpu.SMEM), vmem),
        scratch_shapes=[
            pltpu.VMEM((owners, slots), f32),
            pltpu.VMEM((2 * owners, full), f32),
            pltpu.VMEM((users, slots), i32),
        ],
        compiler_params=pltpu.CompilerParams(vmem_limit_bytes=32 * MIB),
    )(owner, row)


def split3(x):
    high = x.astype(bf16)
    rest = x - high.astype(f32)
    mid = rest.astype(bf16)
    low = (rest - mid.astype(f32)).astype(bf16)
    return high, mid, low


def conjugate(big, target, vec):
    rank, users = target.shape

    def apply_system():
        def part(index, acc):
            return acc + big[pl.ds(pl.multiple_of(index * rank, rank), rank), :] * vec[pl.ds(index, 1), :]
        return lax.fori_loop(0, rank, part, jnp.zeros((rank, users), f32), unroll=8)

    def advance(index, carry):
        solution, residual, norm_now = carry
        image = apply_system()
        direction = vec[...]
        alpha = norm_now / (jnp.sum(direction * image, axis=0, keepdims=True) + tiny)
        solution = solution + alpha * direction
        residual = residual - alpha * image
        norm_next = jnp.sum(residual * residual, axis=0, keepdims=True)
        vec[...] = residual + norm_next / (norm_now + tiny) * direction
        return solution, residual, norm_next

    vec[...] = target
    start = (jnp.zeros_like(target), target, jnp.sum(target * target, axis=0, keepdims=True))
    return lax.fori_loop(0, ITERS, advance, start)[0]


def solve_kernel(gram_scale, place, fetched, strength, gram, out, wide, rows, systems, big, targets, vec):
    users, slots = strength.shape
    rank = out.shape[1]
    fetch_total = wide.shape[0]
    step = max(size for size in range(16, 1200, 16) if fetch_total % size == 0)

    def widen(index, _):
        at = pl.ds(pl.multiple_of(index * step, step), step)
        wide[at, :] = fetched[at, :].astype(f32)
        return 0

    lax.fori_loop(0, fetch_total // step, widen, 0)
    eye = jnp.where(
        lax.broadcasted_iota(i32, (rank, rank), 0) == lax.broadcasted_iota(i32, (rank, rank), 1), ridge, 0.0
    )
    shared = gram[:rank, :] * gram_scale + eye


    def some_users(index, _):
        helds = []
        for g in range(8):
            user = index * 8 + g
            for slot in range(slots):
                rows[pl.ds(g * slots + slot, 1), :] = wide[pl.ds(place[user * slots + slot], 1), :]
        for g in range(8):
            user = index * 8 + g
            held = rows[g * slots:(g + 1) * slots, :]
            short = held.astype(bf16)
            weights = strength[pl.ds(user, 1), :]
            turned = short.T.astype(f32)
            parts = split3(turned * weights)[:3]
            extra = split3(jnp.broadcast_to(1.0 + weights, (16, slots)))
            left = jnp.concatenate([*parts, *extra], axis=0)
            product = jnp.dot(left, short, preferred_element_type=f32)
            system = product[(3 - 1) * rank:3 * rank]
            for k in range(3 - 2, -1, -1):
                system = system + product[k * rank:(k + 1) * rank]
            systems[pl.ds(pl.multiple_of(user * rank, rank), rank), :] = system + shared
            tail = 3 * rank
            targets[pl.ds(user, 1), :] = (
                product[tail:tail + 1] + (product[tail + 16:tail + 17] + product[tail + 32:tail + 33])
            )
        return 0

    lax.fori_loop(0, users // 8, some_users, 0)

    def turn(index, _):
        block = systems[pl.ds(index, users, stride=rank), :]
        big[pl.ds(pl.multiple_of(index * rank, rank), rank), :] = block.T
        return 0

    lax.fori_loop(0, rank, turn, 0, unroll=8)
    out[...] = conjugate(big, targets[...].T, vec).T


def solve(place, fetched, strength, gram, gram_scale):
    users, slots = strength.shape
    total, rank = fetched.shape
    vmem = pl.BlockSpec(memory_space=pltpu.VMEM)
    return pl.pallas_call(
        functools.partial(solve_kernel, gram_scale),
        out_shape=jax.ShapeDtypeStruct((users, rank), f32),
        in_specs=[pl.BlockSpec(memory_space=pltpu.SMEM), vmem, vmem, vmem],
        out_specs=vmem,
        scratch_shapes=[
            pltpu.VMEM((total, rank), f32),
            pltpu.VMEM((8 * slots, rank), f32),
            pltpu.VMEM((users * rank, rank), f32),
            pltpu.VMEM((rank * rank, users), f32),
            pltpu.VMEM((users, rank), f32),
            pltpu.VMEM((rank, users), f32),
        ],
        compiler_params=pltpu.CompilerParams(vmem_limit_bytes=60 * MIB),
    )(place, fetched, strength, gram)


MESH = pl.DeviceIdType.MESH
LANES = 128
PIECE = 8


def exchange_kernel(cap, spare, near, asked, hot, wrong, table, out, sums, got, idx, wide, block, send,
                    gram_send, gram_got, gram_far, core_buf, core_send, y_send, y_buf, z_send, z_buf, last,
                    ask_send, ask_recv, row_send, row_recv, gram_sems, sum_sems, far_sems, hop_sems, copy_sems):
    me, copy_id = lax.axis_index("rows"), lax.axis_index("grp")
    copies = lax.axis_size("grp")
    n = asked.shape[0]
    z, y, c = me // 8, (me // 2) % 4, me % 2
    full = cap + spare

    def offset(step):
        k = step % 8
        dz = (k + 1) // 2 * (1 - 2 * (k % 2))
        return (dz + 8) % 8, (step // 8) % 4, step // 32

    def index_of(pz, py, pc):
        return (pz * 4 + py) * 2 + pc

    def ahead(step):
        dz, dy, dc = offset(step)
        return index_of((z + dz) % 8, (y + dy) % 4, (c + dc) % 2)

    def behind(step):
        dz, dy, dc = offset(step)
        return index_of((z + 8 - dz) % 8, (y + 4 - dy) % 4, (c + 2 - dc) % 2)

    def loop(low, high, body):
        def run(step, _):
            body(step)
            return 0
        lax.fori_loop(low, high, run, 0)

    def remote(src, dst, first, second, **device_id):
        return pltpu.make_async_remote_copy(
            src_ref=src, dst_ref=dst, send_sem=first, recv_sem=second,
            device_id=device_id, device_id_type=MESH)

    barrier = pltpu.get_barrier_semaphore()
    loop(1, n, lambda step: pl.semaphore_signal(
        barrier, inc=1, device_id={"rows": ahead(step)}, device_id_type=MESH))
    loop(1, copies, lambda step: pl.semaphore_signal(
        barrier, inc=1, device_id={"grp": (copy_id + step) % copies}, device_id_type=MESH))
    pl.semaphore_wait(barrier, n + copies - 2)

    def ask(step):
        return remote(asked.at[ahead(step)], got.at[step], ask_send.at[step], ask_recv.at[step], rows=ahead(step))

    loop(1, n, lambda step: ask(step).start())
    mine = pltpu.make_async_copy(asked.at[me], got.at[0], copy_sems.at[0])
    mine.start()

    share = table.shape[0] // copies
    part = 512

    def gram_part(index, acc):
        rows = table[pl.ds(pl.multiple_of(copy_id * share + index * part, part), part), :]
        return acc + lax.dot_general(rows, rows, (((0,), (0,)), ((), ())), preferred_element_type=f32)

    rank = table.shape[1]
    gram_send[:rank, :] = lax.fori_loop(0, share // part, gram_part, jnp.zeros((rank, rank), f32))
    gram_send[rank:, :] = wrong[...]
    pieces = gram_send.shape[0] // PIECE

    def piece(ref, index):
        return ref.at[pl.ds(pl.multiple_of(index * PIECE, PIECE), PIECE)]

    def gram_out(index):
        return remote(piece(gram_send, index), gram_got.at[me], gram_sems.at[0, index], gram_sems.at[1, me], rows=3 * index)

    def gram_start(index):
        @pl.when(3 * index != me)
        def _():
            gram_out(index).start()

    loop(0, pieces, gram_start)

    def widen(index):
        at = pl.ds(pl.multiple_of(index * part, part), part)
        wide[at, :] = table[at, :].astype(f32)

    loop(0, table.shape[0] // part, widen)
    loop(1, n, lambda step: ask(step).wait_recv())
    mine.wait()
    numbers = pltpu.make_async_copy(got, idx, copy_sems.at[0])
    numbers.start()
    numbers.wait()

    def fetch(step, line, first, count, dst, at):
        for inner in range(count):
            block[pl.ds(inner, 1), :] = wide[pl.ds(idx[step, line, first + inner], 1), :]
        dst[pl.ds(at, count), :] = block[:count, :].astype(bf16)

    lines, rest = cap // LANES, cap % LANES

    def serve_rows(step):
        loop(0, lines, lambda line: fetch(
            step, line, 0, LANES, send.at[step], pl.multiple_of(line * LANES, LANES)))
        if rest:
            fetch(step, lines, 0, rest, send.at[step], lines * LANES)

    def answer(step):
        return remote(send.at[step], out.at[pl.ds(pl.multiple_of(me * cap, 16), cap)],
                      row_send.at[step], row_recv.at[step], rows=behind(step))

    def answered(step):
        return remote(send.at[step], out.at[pl.ds(pl.multiple_of(ahead(step) * cap, 16), cap)],
                      row_send.at[step], row_recv.at[step], rows=ahead(step))

    def serve(step):
        serve_rows(step)
        answer(step).start()

    def spare_rows(step, dst):
        at = 0
        line, first = lines, rest
        while at < spare:
            count = min(LANES - first, spare - at)
            fetch(step, line, first, count, dst, at)
            at, line, first = at + count, line + 1, 0

    def column(step):
        dz, dy, dc = offset(step)
        return ((y + 4 - dy) % 4) * 8 + (z + 8 - dz) % 8

    half = n // 2
    loop(1, near, serve)
    loop(half, n, lambda step: spare_rows(step, core_send.at[column(step)]))
    core_hop = remote(core_send, core_buf.at[c], hop_sems.at[0], hop_sems.at[1], rows=index_of(z, y, 1 - c))
    core_hop.start()
    loop(0, half, lambda step: spare_rows(step, core_buf.at[c, column(step)]))
    loop(near, n, serve)
    serve_rows(0)
    own = pltpu.make_async_copy(send.at[0], out.at[pl.ds(pl.multiple_of(me * cap, 16), cap)], copy_sems.at[0])
    own.start()

    named = hot[0, 0]
    hot_z, hot_y, hot_c = named // 8, (named // 2) % 4, named % 2

    core_hop.wait()

    def keep_core(index):
        y_send[index] = core_buf[hot_c, index]

    loop(0, half, keep_core)

    def y_hop(dy):
        py = (y + dy) % 4
        return remote(y_send.at[pl.ds(py * 8, 8)], y_buf.at[pl.ds(y * 8, 8)], hop_sems.at[2 * dy], hop_sems.at[2 * dy + 1],
                      rows=index_of(z, py, c))

    for dy in (1, 2, 3):
        y_hop(dy).start()

    owner = (me % 3 == 0) & (me < 3 * pieces)

    @pl.when(owner)
    def _():
        gram_got[me] = gram_send[pl.ds(pl.multiple_of(me // 3 * PIECE, PIECE), PIECE), :]

        def gram_in(index):
            @pl.when(index != me)
            def _():
                remote(piece(gram_send, 0), gram_got.at[index], gram_sems.at[0, 0], gram_sems.at[1, index],
                       rows=index).wait_recv()

        loop(0, n, gram_in)
        gram_far[copy_id] = lax.fori_loop(
            0, n, lambda index, acc: acc + gram_got[index], jnp.zeros((PIECE, rank), f32))

        def far(step):
            return remote(gram_far.at[copy_id], gram_far.at[copy_id], far_sems.at[0, step], far_sems.at[1, step],
                          grp=(copy_id + step) % copies)

        for step in range(1, 4):
            far(step).start()
        for step in range(1, 4):
            far(step).wait()
        total = gram_far[0]
        for index in range(1, 4):
            total = total + gram_far[index]
        sums[pl.ds(pl.multiple_of(me // 3 * PIECE, PIECE), PIECE), :] = total

    def spread(step):
        at = piece(sums, me // 3)
        return remote(at, at, sum_sems.at[0, step], sum_sems.at[1, me // 3], rows=ahead(step))

    @pl.when(owner)
    def _():
        loop(1, n, lambda step: spread(step).start())

    for dy in (1, 2, 3):
        y_hop(dy).wait()

    def keep_y(index):
        y_buf[y * 8 + index] = y_send[y * 8 + index]

    loop(0, 8, keep_y)

    def keep_z(index):
        z_send[index] = y_buf[hot_y * 8 + index]

    loop(0, 8, keep_z)

    def z_hop(dz):
        pz = (z + dz) % 8
        return remote(z_send.at[pz], z_buf.at[z], hop_sems.at[8 + 2 * dz], hop_sems.at[9 + 2 * dz],
                      rows=index_of(pz, y, c))

    loop(1, 8, lambda dz: z_hop(dz).start())
    z_buf[z] = z_send[z]

    def finish(step):
        ask(step).wait_send()
        answer(step).wait_send()
        answered(step).wait_recv()

    loop(1, n, finish)
    loop(1, 8, lambda dz: z_hop(dz).wait())
    own.wait()
    last[...] = z_buf[hot_z]
    tail = pltpu.make_async_copy(last, out.at[pl.ds(n * cap, spare)], copy_sems.at[0])
    tail.start()
    tail.wait()

    def gram_sent(index):
        @pl.when(3 * index != me)
        def _():
            gram_out(index).wait_send()
            at = piece(sums, index)
            remote(at, at, sum_sems.at[0, 0], sum_sems.at[1, index], rows=3 * index).wait_recv()

    loop(0, pieces, gram_sent)

    @pl.when(owner)
    def _():
        loop(1, n, lambda step: spread(step).wait_send())


def exchange(asked, hot, wrong, table, cap, spare, copies, near):
    owners, lines, _ = asked.shape
    rows, rank = table.shape
    vmem = pl.BlockSpec(memory_space=pltpu.VMEM)
    dma = pltpu.SemaphoreType.DMA
    half = owners // 2
    pieces = rank // PIECE + 1
    return pl.pallas_call(
        functools.partial(exchange_kernel, cap, spare, near),
        out_shape=(
            jax.ShapeDtypeStruct((owners * cap + spare, rank), bf16),
            jax.ShapeDtypeStruct((pieces * PIECE, rank), f32),
        ),
        in_specs=[vmem, pl.BlockSpec(memory_space=pltpu.SMEM), vmem, vmem],
        out_specs=(pl.BlockSpec(memory_space=pl.ANY), vmem),
        scratch_shapes=[
            pltpu.VMEM((owners, lines, LANES), i32),
            pltpu.SMEM((owners, lines, LANES), i32),
            pltpu.VMEM((rows, rank), f32),
            pltpu.VMEM((LANES, rank), f32),
            pltpu.VMEM((owners, cap, rank), bf16),
            pltpu.VMEM((pieces * PIECE, rank), f32),
            pltpu.VMEM((owners, PIECE, rank), f32),
            pltpu.VMEM((copies, PIECE, rank), f32),
            pltpu.VMEM((2, half, spare, rank), bf16),
            pltpu.VMEM((half, spare, rank), bf16),
            pltpu.VMEM((half, spare, rank), bf16),
            pltpu.VMEM((half, spare, rank), bf16),
            pltpu.VMEM((8, spare, rank), bf16),
            pltpu.VMEM((8, spare, rank), bf16),
            pltpu.VMEM((spare, rank), bf16),
            dma((owners,)), dma((owners,)), dma((owners,)), dma((owners,)),
            dma((2, owners)), dma((2, owners)), dma((2, 4)), dma((24,)), dma((1,)),
        ],
        compiler_params=pltpu.CompilerParams(collective_id=0, has_side_effects=True, vmem_limit_bytes=48 * MIB),
    )(asked, hot, wrong, table)


def fetch_any(item_factors, rated_owner, rated_row):
    owners = lax.axis_size("rows")
    slot_owner = rated_owner.reshape(-1)
    local_row = rated_row.reshape(-1)
    slot_total = slot_owner.shape[0]
    rank = item_factors.shape[1]
    capacity = 2 * slot_total // owners
    slot_order = jnp.argsort(slot_owner, stable=True)
    sorted_owner = slot_owner[slot_order]
    owner_starts = jnp.searchsorted(sorted_owner, jnp.arange(owners, dtype=jnp.int32))
    sorted_rank = jnp.arange(slot_total, dtype=jnp.int32) - owner_starts[sorted_owner]
    sorted_place = sorted_owner * capacity + sorted_rank
    bucket_slot = jnp.zeros((slot_total,), jnp.int32).at[slot_order].set(sorted_place)
    asked_rows = jnp.zeros((owners * capacity,), jnp.int32).at[bucket_slot].set(local_row)
    asked_rows = asked_rows.reshape(owners, capacity)
    found = jnp.take(
        item_factors,
        lax.all_to_all(asked_rows, "rows", split_axis=0, concat_axis=0, tiled=True),
        axis=0,
    )
    fetched = lax.all_to_all(found, "rows", split_axis=0, concat_axis=0, tiled=True)
    return jnp.take(fetched.reshape(owners * capacity, rank), bucket_slot, axis=0)


def per_device(item_factors, rated_owner, rated_row, strength):
    user_count, slot_count = rated_owner.shape
    shard_rows, rank = item_factors.shape
    owners = lax.axis_size("rows")
    most = 2 * user_count * slot_count // owners
    cap = most * CAP_PART // 8
    place, asked, hot, wrong = prepare(rated_owner, rated_row, owners, cap, most - cap)
    fetched, sums = exchange(asked, hot, wrong, item_factors, cap, most - cap, lax.axis_size("grp"), NEAR)
    scale = slot_count / (shard_rows * owners)

    def usual(_):
        return solve(place.reshape(-1), fetched, strength, sums, scale)

    def any_counts(_):
        rows = fetch_any(item_factors, rated_owner, rated_row)
        return solve(jnp.arange(user_count * slot_count, dtype=jnp.int32), rows, strength, sums, scale)

    return lax.cond(sums[rank, 0] == 0.0, usual, any_counts, 0)


def solution(mesh):
    placed = (P("rows", None), P(("rows", "grp"), None), P(("rows", "grp"), None), P(("rows", "grp"), None))
    return jax.shard_map(
        per_device, mesh=mesh, in_specs=placed, out_specs=P(("rows", "grp"), None), check_vma=False
    )
```

time: 386 us -> 217 us (0.56)
  waiting for transfers between devices: 88.6 us -> 0 us
  Pallas kernels: 275 us -> 213 us
  between operations: 13.4 us -> 0.7 us
    psum x1 -> x0, waiting for transfers between devices: 88.6 us -> none  [per_device(): gram_total = lax.psum(partial_gram, ('rows', 'grp'))]
    pallas_call x3, Pallas kernels: 275 us -> 213 us  [the longest x1 161 us: exchange(): pl.pallas_call(functools.partial(exchange_kernel, cap, spare, near), out_...]
  transfers between devices with their start and end apart: 1 -> 0, of which waited for: 1 -> 0; matrix products, arithmetic and copies ran while one was open for 0% -> 0% of each run, Pallas kernels for 60% -> 0%
where the time goes in v2:
time: 217 us; the launch traced here: 215 us
  Pallas kernels  213 us (98%)
    pallas_call x1, Pallas kernels, exchange(): pl.pallas_call(functools.partial(exchange_kernel, cap, spare, near), out_...  161 us
    pallas_call x1, Pallas kernels, solve(): pl.pallas_call(functools.partial(solve_kernel, gram_scale), out_shape=jax...  41.7 us
    pallas_call x1, Pallas kernels, prepare(): pl.pallas_call(functools.partial(prep_kernel, owners, cap, spare, group),...  10.3 us

profile of v2, /device:TPU:1, one launch (start us, length us, event | category | flops | bytes accessed | tf_op | source)
XLA Modules:
  0.0 215.1 jit_solution(8512970218652764686)
XLA Ops:
  0.0 0.0 copy-start
  0.0 0.0 copy-start.1
  0.0 10.3 %shard_map.48 = (s32[128,128]{1,0:T(8,128)S(1)}, s32[64,4,128]{2,1,0:T(4,128)S(1)}, s32[1,1]{1,0:T(1,128)}, f32[8,128]{1,0:T(8,128)S(1)}) custom-call(s32[128,128]{1,0:T(8,128)} %owner_ref.1, s32[128,128]{1,0:T(8,128)} %row_ref.1), custom_call_target="tpu_custom_call" | custom-call | tf_op jit(solution)/shard_map/pallas_call | solution.py:73
  10.3 161.1 %shard_map.49 = (bf16[20672,128]{1,0:T(8,128)(2,1)}, f32[136,128]{1,0:T(8,128)S(1)}) custom-call(s32[64,4,128]{2,1,0:T(4,128)S(1)} %get-tuple-element.107.asked, s32[1,1]{1,0:T(1,128)} %get-tuple-element.108.hot, f32[8,128]{1,0:T(8,128)S(1)} %get-tuple-element.109.wrong, bf16[16384,128]{1,0:T(8,128)(2,1)} %table.1), custom_call_target="tpu_custom_call" | custom-call | tf_op jit(solution)/shard_map/pallas_call | solution.py:449
  171.4 0.5 slice.3
  172.6 0.0 copy-done
  172.6 0.0 copy-done.1
  172.6 41.9 %conditional.1 = (f32[128,128]{1,0:T(8,128)S(1)}) conditional(s32[]{:T(128)} %bitcast.74, (s32[128,128]{1,0:T(8,128)S(1)}, s32[128,128]{1,0:T(8,128)}, bf16[16384,128]{1,0:T(8,128)(2,1)}, f32[128,128]{1,0:T(8,128)S(1)}, f32[136,128]{1,0:T(8,128)S(1)}) %tuple.167, (s32[128,128]{1,0:T(8,128)S(1)}, bf16[20672,128]{1,0:T(8,128)(2,1)}, ...), branch_computations={%region_0.6_spmd, %region_6.7_spmd} | conditional | flops 9242500 | bytes 80290768 | solution.py:521
  172.8 41.7 %branch_1_fun.1 = f32[128,128]{1,0:T(8,128)S(1)} custom-call(s32[16384]{0:T(1024)S(1)} %bitcast.87, bf16[20672,128]{1,0:T(8,128)(2,1)} %get-tuple-element.98.fetched, f32[128,128]{1,0:T(8,128)S(1)} %get-tuple-element.99.strength, f32[136,128]{1,0:T(8,128)S(1)} %get-tuple-element.100.gram), custom_call_target="tpu_custom_call" | custom-call | tf_op jit(solution)/shard_map/cond/branch_1_fun/pallas_call | solution.py:183
  214.5 0.0 copy-start.2
  214.5 0.6 copy-done.2
Async XLA Ops:
  0.0 172.6 %copy-start = (s32[128,128]{1,0:T(8,128)S(1)}, s32[128,128]{1,0:T(8,128)}, u32[]{:S(2)}) copy-start(s32[128,128]{1,0:T(8,128)} %owner_ref.1) | copy-start | bytes 196612
  0.0 172.6 %copy-start.1 = (f32[128,128]{1,0:T(8,128)S(1)}, f32[128,128]{1,0:T(8,128)}, u32[]{:S(2)}) copy-start(f32[128,128]{1,0:T(8,128)} %param.11) | copy-start | bytes 196612
  214.5 0.6 copy-start.2

commit v3 on v2

--- a/solution.py
+++ b/solution.py
@@ -13,12 +13,13 @@
 MIB = 1024 * 1024
 
 
-CAP_PART = 5
-NEAR = 24
-
-
-def prep_kernel(owners, cap, spare, group, owner_ref, row_ref, place_ref, asked_ref, hot_ref, wrong_ref, base, acc, ranks):
+NEAR = (12, 24, 40, 64, 48)
+GROUP = 8
+
+
+def prep_kernel(owners, early, late, spare, early_users, group, owner_ref, row_ref, place_ref, asked_ref, hot_ref, wrong_ref, base, acc, ranks):
     users, slots = owner_ref.shape
+    cap = early + late
     full = cap + spare
     which = lax.broadcasted_iota(i32, (owners, slots), 0)
     before = lax.broadcasted_iota(i32, (slots, 2 * slots), 0)
@@ -56,22 +57,38 @@
     hot = jnp.min(jnp.where(counts == jnp.max(counts), which, owners))
     hot_ref[0, 0] = hot
     own, rank = owner_ref[...], ranks[...]
-    past = rank >= cap
-    place_ref[...] = jnp.where(past & (own == hot), owners * cap - cap + rank, own * cap + jnp.minimum(rank, cap - 1))
-    bad = jnp.sum(jnp.where(past & (own != hot), 1.0, 0.0))
+    favoured = own == hot
+    user = lax.broadcasted_iota(i32, rank.shape, 0)
+    first = user < early_users
+    spot = jnp.where(
+        favoured & (rank >= early),
+        jnp.where(rank < early + spare, rank + late, rank - spare),
+        jnp.where(favoured, rank, jnp.minimum(rank, cap - 1)),
+    )
+    late_base = owners * early
+    place_ref[...] = jnp.where(
+        spot < early,
+        own * early + spot,
+        jnp.where(spot < cap, late_base + own * late + spot - early, late_base + owners * late + spot - cap),
+    )
+    limit = jnp.where(
+        favoured, jnp.where(first, early + spare, full), jnp.where(first, early, cap))
+    bad = jnp.sum(jnp.where(rank >= limit, 1.0, 0.0))
     wrong_ref[...] = jnp.zeros_like(wrong_ref) + bad
     total = acc[...]
     asked = (total[:owners] * 128.0 + total[owners:]).astype(i32)
+    moved = jnp.concatenate([asked[:, :early], asked[:, early + spare:], asked[:, early:early + spare]], axis=1)
+    asked = jnp.where(lax.broadcasted_iota(i32, asked.shape, 0) == hot, moved, asked)
     for line in range(full // 128):
         asked_ref[:, line, :] = asked[:, line * 128:(line + 1) * 128]
 
 
-def prepare(owner, row, owners, cap, spare, group=16):
+def prepare(owner, row, owners, early, late, spare, early_users, group=16):
     users, slots = owner.shape
-    full = cap + spare
+    full = early + late + spare
     vmem = pl.BlockSpec(memory_space=pltpu.VMEM)
     return pl.pallas_call(
-        functools.partial(prep_kernel, owners, cap, spare, group),
+        functools.partial(prep_kernel, owners, early, late, spare, early_users, group),
         out_shape=(
             jax.ShapeDtypeStruct((users, slots), i32),
             jax.ShapeDtypeStruct((owners, full // 128, 128), i32),
@@ -121,59 +138,67 @@
     return lax.fori_loop(0, ITERS, advance, start)[0]
 
 
-def solve_kernel(gram_scale, place, fetched, strength, gram, out, wide, rows, systems, big, targets, vec):
-    users, slots = strength.shape
-    rank = out.shape[1]
-    fetch_total = wide.shape[0]
-    step = max(size for size in range(16, 1200, 16) if fetch_total % size == 0)
-
-    def widen(index, _):
-        at = pl.ds(pl.multiple_of(index * step, step), step)
-        wide[at, :] = fetched[at, :].astype(f32)
+def widen_rows(source, target, base):
+    total = source.shape[0]
+    size = max(part for part in range(16, 1040, 16) if total % part == 0)
+
+    def part(index, _):
+        at = pl.multiple_of(index * size, size)
+        target[pl.ds(base + at, size), :] = source[pl.ds(at, size), :].astype(f32)
         return 0
 
-    lax.fori_loop(0, fetch_total // step, widen, 0)
-    eye = jnp.where(
-        lax.broadcasted_iota(i32, (rank, rank), 0) == lax.broadcasted_iota(i32, (rank, rank), 1), ridge, 0.0
-    )
-    shared = gram[:rank, :] * gram_scale + eye
-
+    lax.fori_loop(0, total // size, part, 0)
+
+
+def gram_shared(sums, scale):
+    rank = sums.shape[1]
+    same = lax.broadcasted_iota(i32, (rank, rank), 0) == lax.broadcasted_iota(i32, (rank, rank), 1)
+    return sums[:rank, :] * scale + jnp.where(same, ridge, 0.0)
+
+
+def build_systems(first, last, place, wide, strength, rows, systems, targets):
+    slots, rank = strength.shape[1], systems.shape[1]
 
     def some_users(index, _):
-        helds = []
-        for g in range(8):
-            user = index * 8 + g
+        for g in range(GROUP):
+            user = index * GROUP + g
             for slot in range(slots):
                 rows[pl.ds(g * slots + slot, 1), :] = wide[pl.ds(place[user * slots + slot], 1), :]
-        for g in range(8):
-            user = index * 8 + g
-            held = rows[g * slots:(g + 1) * slots, :]
-            short = held.astype(bf16)
+        for g in range(GROUP):
+            user = index * GROUP + g
+            short = rows[g * slots:(g + 1) * slots, :].astype(bf16)
             weights = strength[pl.ds(user, 1), :]
-            turned = short.T.astype(f32)
-            parts = split3(turned * weights)[:3]
             extra = split3(jnp.broadcast_to(1.0 + weights, (16, slots)))
-            left = jnp.concatenate([*parts, *extra], axis=0)
+            left = jnp.concatenate([*split3(short.T.astype(f32) * weights), *extra], axis=0)
             product = jnp.dot(left, short, preferred_element_type=f32)
-            system = product[(3 - 1) * rank:3 * rank]
-            for k in range(3 - 2, -1, -1):
-                system = system + product[k * rank:(k + 1) * rank]
-            systems[pl.ds(pl.multiple_of(user * rank, rank), rank), :] = system + shared
+            system = product[2 * rank:3 * rank] + product[rank:2 * rank] + product[:rank]
+            systems[pl.ds(pl.multiple_of(user * rank, rank), rank), :] = system
             tail = 3 * rank
             targets[pl.ds(user, 1), :] = (
                 product[tail:tail + 1] + (product[tail + 16:tail + 17] + product[tail + 32:tail + 33])
             )
         return 0
 
-    lax.fori_loop(0, users // 8, some_users, 0)
+    lax.fori_loop(first // GROUP, last // GROUP, some_users, 0)
+
+
+def solve_systems(shared, systems, big, targets, vec):
+    users, rank = targets.shape
 
     def turn(index, _):
-        block = systems[pl.ds(index, users, stride=rank), :]
+        block = systems[pl.ds(index, users, stride=rank), :] + shared[pl.ds(index, 1), :]
         big[pl.ds(pl.multiple_of(index * rank, rank), rank), :] = block.T
         return 0
 
     lax.fori_loop(0, rank, turn, 0, unroll=8)
-    out[...] = conjugate(big, targets[...].T, vec).T
+    return conjugate(big, targets[...].T, vec).T
+
+
+def solve_kernel(scale, place, fetched, strength, sums, out, wide, shared, rows, systems, big, targets, vec):
+    widen_rows(fetched, wide, 0)
+    build_systems(0, strength.shape[0], place, wide, strength, rows, systems, targets)
+    shared[...] = gram_shared(sums, scale)
+    out[...] = solve_systems(shared, systems, big, targets, vec)
 
 
 def solve(place, fetched, strength, gram, gram_scale):
@@ -187,6 +212,7 @@
         out_specs=vmem,
         scratch_shapes=[
             pltpu.VMEM((total, rank), f32),
+            pltpu.VMEM((rank, rank), f32),
             pltpu.VMEM((8 * slots, rank), f32),
             pltpu.VMEM((users * rank, rank), f32),
             pltpu.VMEM((rank * rank, users), f32),
@@ -202,14 +228,21 @@
 PIECE = 8
 
 
-def exchange_kernel(cap, spare, near, asked, hot, wrong, table, out, sums, got, idx, wide, block, send,
-                    gram_send, gram_got, gram_far, core_buf, core_send, y_send, y_buf, z_send, z_buf, last,
-                    ask_send, ask_recv, row_send, row_recv, gram_sems, sum_sems, far_sems, hop_sems, copy_sems):
+def exchange_kernel(early, late, spare, early_users, near, scale, asked, hot, wrong, place_in, strength, table_in,
+                    out, sums, got, idx, place, table, wide, block, send_early, send_late, got_early, got_late,
+                    gram_send, gram_got, gram_far, core_buf, core_send, y_send, y_buf, z_send, z_buf,
+                    fetched, rows, systems, targets, vec,
+                    ask_send, ask_recv, early_send, early_recv, late_send, late_recv, gram_sems, sum_sems, far_sems,
+                    hop_sems, copy_sems):
     me, copy_id = lax.axis_index("rows"), lax.axis_index("grp")
     copies = lax.axis_size("grp")
     n = asked.shape[0]
     z, y, c = me // 8, (me // 2) % 4, me % 2
-    full = cap + spare
+    cap = early + late
+    table_copy = pltpu.make_async_copy(table_in, table, copy_sems.at[1])
+    table_copy.start()
+    place_copy = pltpu.make_async_copy(place_in, place, copy_sems.at[2])
+    place_copy.start()
 
     def offset(step):
         k = step % 8
@@ -252,6 +285,7 @@
     mine = pltpu.make_async_copy(asked.at[me], got.at[0], copy_sems.at[0])
     mine.start()
 
+    table_copy.wait()
     share = table.shape[0] // copies
     part = 512
 
@@ -277,45 +311,50 @@
 
     loop(0, pieces, gram_start)
 
-    def widen(index):
-        at = pl.ds(pl.multiple_of(index * part, part), part)
-        wide[at, :] = table[at, :].astype(f32)
-
-    loop(0, table.shape[0] // part, widen)
+    widen_rows(table, wide, 0)
     loop(1, n, lambda step: ask(step).wait_recv())
     mine.wait()
-    numbers = pltpu.make_async_copy(got, idx, copy_sems.at[0])
-    numbers.start()
-    numbers.wait()
+    first_steps = 16
+
+    def numbers(low, count, sem):
+        return pltpu.make_async_copy(got.at[pl.ds(low, count)], idx.at[pl.ds(low, count)], copy_sems.at[sem])
+
+    numbers(0, first_steps, 0).start()
+    numbers(first_steps, n - first_steps, 3).start()
+    numbers(0, first_steps, 0).wait()
 
     def fetch(step, line, first, count, dst, at):
         for inner in range(count):
             block[pl.ds(inner, 1), :] = wide[pl.ds(idx[step, line, first + inner], 1), :]
         dst[pl.ds(at, count), :] = block[:count, :].astype(bf16)
 
-    lines, rest = cap // LANES, cap % LANES
-
-    def serve_rows(step):
-        loop(0, lines, lambda line: fetch(
-            step, line, 0, LANES, send.at[step], pl.multiple_of(line * LANES, LANES)))
-        if rest:
-            fetch(step, lines, 0, rest, send.at[step], lines * LANES)
-
-    def answer(step):
-        return remote(send.at[step], out.at[pl.ds(pl.multiple_of(me * cap, 16), cap)],
-                      row_send.at[step], row_recv.at[step], rows=behind(step))
-
-    def answered(step):
-        return remote(send.at[step], out.at[pl.ds(pl.multiple_of(ahead(step) * cap, 16), cap)],
-                      row_send.at[step], row_recv.at[step], rows=ahead(step))
+    def serve_early(step):
+        loop(0, early // LANES, lambda line: fetch(
+            step, line, 0, LANES, send_early.at[step], pl.multiple_of(line * LANES, LANES)))
+
+    def serve_late(step):
+        fetch(step, early // LANES, 0, late, send_late.at[step], 0)
+
+    def early_to(step):
+        return remote(send_early.at[step], got_early.at[me], early_send.at[step], early_recv.at[step], rows=behind(step))
+
+    def early_from(step):
+        return remote(send_early.at[step], got_early.at[ahead(step)], early_send.at[step], early_recv.at[step],
+                      rows=ahead(step))
+
+    def late_to(step):
+        return remote(send_late.at[step], got_late.at[me], late_send.at[step], late_recv.at[step], rows=behind(step))
+
+    def late_from(step):
+        return remote(send_late.at[step], got_late.at[ahead(step)], late_send.at[step], late_recv.at[step],
+                      rows=ahead(step))
 
     def serve(step):
-        serve_rows(step)
-        answer(step).start()
+        serve_early(step)
+        early_to(step).start()
 
     def spare_rows(step, dst):
-        at = 0
-        line, first = lines, rest
+        at, line, first = 0, cap // LANES, cap % LANES
         while at < spare:
             count = min(LANES - first, spare - at)
             fetch(step, line, first, count, dst, at)
@@ -326,16 +365,15 @@
         return ((y + 4 - dy) % 4) * 8 + (z + 8 - dz) % 8
 
     half = n // 2
-    loop(1, near, serve)
+    one, two, three, four, ahead_of = near
+    loop(1, one, serve)
+    numbers(first_steps, n - first_steps, 3).wait()
     loop(half, n, lambda step: spare_rows(step, core_send.at[column(step)]))
     core_hop = remote(core_send, core_buf.at[c], hop_sems.at[0], hop_sems.at[1], rows=index_of(z, y, 1 - c))
     core_hop.start()
+    loop(one, two, serve)
     loop(0, half, lambda step: spare_rows(step, core_buf.at[c, column(step)]))
-    loop(near, n, serve)
-    serve_rows(0)
-    own = pltpu.make_async_copy(send.at[0], out.at[pl.ds(pl.multiple_of(me * cap, 16), cap)], copy_sems.at[0])
-    own.start()
-
+    loop(two, three, serve)
     named = hot[0, 0]
     hot_z, hot_y, hot_c = named // 8, (named // 2) % 4, named % 2
 
@@ -353,6 +391,47 @@
 
     for dy in (1, 2, 3):
         y_hop(dy).start()
+
+    loop(three, four, serve)
+    for dy in (1, 2, 3):
+        y_hop(dy).wait()
+
+    def keep_y(index):
+        y_buf[y * 8 + index] = y_send[y * 8 + index]
+
+    loop(0, 8, keep_y)
+
+    def keep_z(index):
+        z_send[index] = y_buf[hot_y * 8 + index]
+
+    loop(0, 8, keep_z)
+
+    def z_hop(dz):
+        pz = (z + dz) % 8
+        return remote(z_send.at[pz], z_buf.at[z], hop_sems.at[8 + 2 * dz], hop_sems.at[9 + 2 * dz],
+                      rows=index_of(pz, y, c))
+
+    loop(1, 8, lambda dz: z_hop(dz).start())
+    z_buf[z] = z_send[z]
+
+    loop(four, n, serve)
+    loop(1, n, serve_late)
+    loop(1, ahead_of, lambda step: early_to(step).wait_send())
+
+    def serve_rest(step):
+        @pl.when(step + ahead_of <= n)
+        def _():
+            early_to(step + ahead_of - 1).wait_send()
+
+        late_to(step).start()
+
+    loop(1, n, serve_rest)
+    serve_early(0)
+    serve_late(0)
+    own_early = pltpu.make_async_copy(send_early.at[0], got_early.at[me], copy_sems.at[0])
+    own_late = pltpu.make_async_copy(send_late.at[0], got_late.at[me], copy_sems.at[1])
+    own_early.start()
+    own_late.start()
 
     owner = (me % 3 == 0) & (me < 3 * pieces)
 
@@ -391,39 +470,7 @@
     def _():
         loop(1, n, lambda step: spread(step).start())
 
-    for dy in (1, 2, 3):
-        y_hop(dy).wait()
-
-    def keep_y(index):
-        y_buf[y * 8 + index] = y_send[y * 8 + index]
-
-    loop(0, 8, keep_y)
-
-    def keep_z(index):
-        z_send[index] = y_buf[hot_y * 8 + index]
-
-    loop(0, 8, keep_z)
-
-    def z_hop(dz):
-        pz = (z + dz) % 8
-        return remote(z_send.at[pz], z_buf.at[z], hop_sems.at[8 + 2 * dz], hop_sems.at[9 + 2 * dz],
-                      rows=index_of(pz, y, c))
-
-    loop(1, 8, lambda dz: z_hop(dz).start())
-    z_buf[z] = z_send[z]
-
-    def finish(step):
-        ask(step).wait_send()
-        answer(step).wait_send()
-        answered(step).wait_recv()
-
-    loop(1, n, finish)
     loop(1, 8, lambda dz: z_hop(dz).wait())
-    own.wait()
-    last[...] = z_buf[hot_z]
-    tail = pltpu.make_async_copy(last, out.at[pl.ds(n * cap, spare)], copy_sems.at[0])
-    tail.start()
-    tail.wait()
 
     def gram_sent(index):
         @pl.when(3 * index != me)
@@ -432,34 +479,68 @@
             at = piece(sums, index)
             remote(at, at, sum_sems.at[0, 0], sum_sems.at[1, index], rows=3 * index).wait_recv()
 
+    own_early.wait()
+    own_late.wait()
+    place_copy.wait()
+    loop(1, n, lambda step: early_from(step).wait_recv())
+
+    def widen_early(index):
+        widen_rows(got_early.at[index], fetched, index * early)
+
+    def widen_late(index):
+        widen_rows(got_late.at[index], fetched, n * early + index * late)
+
+    loop(0, n, widen_early)
+    fetched[pl.ds(n * cap, spare), :] = z_buf[hot_z].astype(f32)
+    users = strength.shape[0]
+    build_systems(0, early_users, place, fetched, strength, rows, systems, targets)
+    loop(1, n, lambda step: late_from(step).wait_recv())
+    loop(0, n, widen_late)
+    build_systems(early_users, users, place, fetched, strength, rows, systems, targets)
     loop(0, pieces, gram_sent)
+    block[...] = gram_shared(sums, scale)
+    out[...] = solve_systems(block, systems, wide, targets, vec)
+
+    def finish(step):
+        ask(step).wait_send()
+        late_to(step).wait_send()
+
+    loop(1, n, finish)
 
     @pl.when(owner)
     def _():
         loop(1, n, lambda step: spread(step).wait_send())
 
 
-def exchange(asked, hot, wrong, table, cap, spare, copies, near):
+def exchange_and_solve(asked, hot, wrong, place, strength, table, early, late, early_users, copies, scale):
     owners, lines, _ = asked.shape
     rows, rank = table.shape
-    vmem = pl.BlockSpec(memory_space=pltpu.VMEM)
+    users, slots = strength.shape
+    cap = early + late
+    spare = lines * LANES - cap
+    vmem, anywhere = pl.BlockSpec(memory_space=pltpu.VMEM), pl.BlockSpec(memory_space=pl.ANY)
     dma = pltpu.SemaphoreType.DMA
     half = owners // 2
     pieces = rank // PIECE + 1
     return pl.pallas_call(
-        functools.partial(exchange_kernel, cap, spare, near),
+        functools.partial(exchange_kernel, early, late, spare, early_users, NEAR, scale),
         out_shape=(
-            jax.ShapeDtypeStruct((owners * cap + spare, rank), bf16),
+            jax.ShapeDtypeStruct((users, rank), f32),
             jax.ShapeDtypeStruct((pieces * PIECE, rank), f32),
         ),
-        in_specs=[vmem, pl.BlockSpec(memory_space=pltpu.SMEM), vmem, vmem],
-        out_specs=(pl.BlockSpec(memory_space=pl.ANY), vmem),
+        in_specs=[vmem, pl.BlockSpec(memory_space=pltpu.SMEM), vmem, anywhere, vmem, anywhere],
+        out_specs=(vmem, vmem),
         scratch_shapes=[
             pltpu.VMEM((owners, lines, LANES), i32),
             pltpu.SMEM((owners, lines, LANES), i32),
+            pltpu.SMEM((users * slots,), i32),
+            pltpu.VMEM((rows, rank), bf16),
             pltpu.VMEM((rows, rank), f32),
             pltpu.VMEM((LANES, rank), f32),
-            pltpu.VMEM((owners, cap, rank), bf16),
+            pltpu.VMEM((owners, early, rank), bf16),
+            pltpu.VMEM((owners, late, rank), bf16),
+            pltpu.VMEM((owners, early, rank), bf16),
+            pltpu.VMEM((owners, late, rank), bf16),
             pltpu.VMEM((pieces * PIECE, rank), f32),
             pltpu.VMEM((owners, PIECE, rank), f32),
             pltpu.VMEM((copies, PIECE, rank), f32),
@@ -469,12 +550,16 @@
             pltpu.VMEM((half, spare, rank), bf16),
             pltpu.VMEM((8, spare, rank), bf16),
             pltpu.VMEM((8, spare, rank), bf16),
-            pltpu.VMEM((spare, rank), bf16),
-            dma((owners,)), dma((owners,)), dma((owners,)), dma((owners,)),
-            dma((2, owners)), dma((2, owners)), dma((2, 4)), dma((24,)), dma((1,)),
+            pltpu.VMEM((owners * cap + spare, rank), f32),
+            pltpu.VMEM((GROUP * slots, rank), f32),
+            pltpu.VMEM((users * rank, rank), f32),
+            pltpu.VMEM((users, rank), f32),
+            pltpu.VMEM((rank, users), f32),
+            dma((owners,)), dma((owners,)), dma((owners,)), dma((owners,)), dma((owners,)), dma((owners,)),
+            dma((2, owners)), dma((2, owners)), dma((2, 4)), dma((24,)), dma((4,)),
         ],
-        compiler_params=pltpu.CompilerParams(collective_id=0, has_side_effects=True, vmem_limit_bytes=48 * MIB),
-    )(asked, hot, wrong, table)
+        compiler_params=pltpu.CompilerParams(collective_id=0, has_side_effects=True, vmem_limit_bytes=60 * MIB),
+    )(asked, hot, wrong, place, strength, table)
 
 
 def fetch_any(item_factors, rated_owner, rated_row):
@@ -506,13 +591,17 @@
     shard_rows, rank = item_factors.shape
     owners = lax.axis_size("rows")
     most = 2 * user_count * slot_count // owners
-    cap = most * CAP_PART // 8
-    place, asked, hot, wrong = prepare(rated_owner, rated_row, owners, cap, most - cap)
-    fetched, sums = exchange(asked, hot, wrong, item_factors, cap, most - cap, lax.axis_size("grp"), NEAR)
+    early, late = most // 2, most // 8
+    early_users = user_count * 3 // 4
+    place, asked, hot, wrong = prepare(
+        rated_owner, rated_row, owners, early, late, most - early - late, early_users)
     scale = slot_count / (shard_rows * owners)
+    solved, sums = exchange_and_solve(
+        asked, hot, wrong, place.reshape(-1), strength, item_factors, early, late, early_users,
+        lax.axis_size("grp"), scale)
 
     def usual(_):
-        return solve(place.reshape(-1), fetched, strength, sums, scale)
+        return solved
 
     def any_counts(_):
         rows = fetch_any(item_factors, rated_owner, rated_row)

time: 217 us -> 194 us (0.89)
  Pallas kernels: 213 us -> 190 us
    pallas_call x3 -> x2, Pallas kernels: 213 us -> 190 us  [the longest x1 180 us: exchange_and_solve(): pl.pallas_call(functools.partial(exchange_kernel, early, late, spare, ear...]
where the time goes in v3:
time: 194 us
  Pallas kernels  190 us (98%)
  local copies, waits for them, and re-layouts  3 us (2%)
    pallas_call x1, Pallas kernels, exchange_and_solve(): pl.pallas_call(functools.partial(exchange_kernel, early, late, spare, ear...  180 us
    pallas_call x1, Pallas kernels, prepare(): pl.pallas_call(functools.partial(prep_kernel, owners, early, late, spare,...  10.3 us

profile of v3, /device:TPU:1, one launch (start us, length us, event | category | flops | bytes accessed | tf_op | source)
XLA Modules:
  0.0 194.0 jit_solution(13229711887603019290)
XLA Ops:
  0.0 0.0 copy-start.3
  0.0 0.0 copy-start.4
  0.0 10.3 %shard_map.48 = (s32[128,128]{1,0:T(8,128)S(1)}, s32[64,4,128]{2,1,0:T(4,128)S(1)}, s32[1,1]{1,0:T(1,128)}, f32[8,128]{1,0:T(8,128)S(1)}) custom-call(s32[128,128]{1,0:T(8,128)} %owner_ref.1, s32[128,128]{1,0:T(8,128)} %row_ref.1), custom_call_target="tpu_custom_call" | custom-call | tf_op jit(solution)/shard_map/pallas_call | solution.py:90
  10.3 0.0 copy-start
  10.3 0.6 copy-done
  11.0 0.0 copy-start.1
  11.0 0.6 copy-done.1
  11.6 0.0 copy-start.2
  11.6 0.6 copy-done.2
  12.2 179.8 %shard_map.49 = (f32[128,128]{1,0:T(8,128)S(1)}, f32[136,128]{1,0:T(8,128)S(1)}) custom-call(s32[64,4,128]{2,1,0:T(4,128)} %copy-done, s32[1,1]{1,0:T(1,128)} %get-tuple-element.97.hot, f32[8,128]{1,0:T(8,128)} %copy-done.2, s32[16384]{0:T(1024)} %bitcast.80, f32[128,128]{1,0:T(8,128)} %strength.1, bf16[16384,128]{1,0:T(8,128)(2,1)} %table_in.1), custom_call_target="tpu_custom_call" | custom-call | tf_op jit(solution)/shard_map/pallas_call | solution.py:525
  192.0 0.5 slice.3
  193.1 0.0 copy-done.3
  193.2 0.0 copy-done.4
  193.2 0.2 conditional.1
  193.4 0.6 copy.23
Async XLA Ops:
  0.0 193.1 %copy-start.3 = (s32[128,128]{1,0:T(8,128)S(1)}, s32[128,128]{1,0:T(8,128)}, u32[]{:S(2)}) copy-start(s32[128,128]{1,0:T(8,128)} %owner_ref.1) | copy-start | bytes 196612
  0.0 193.2 %copy-start.4 = (f32[128,128]{1,0:T(8,128)S(1)}, f32[128,128]{1,0:T(8,128)}, u32[]{:S(2)}) copy-start(f32[128,128]{1,0:T(8,128)} %strength.1) | copy-start | bytes 196612
  10.3 0.6 copy-start
  11.0 0.6 copy-start.1
  11.6 0.6 copy-start.2
